TPU v7x, 32 devices: a whole 2x2x4 slice. The times are simulated.
32 devices in a mesh: groups: 2 (over y), pairs: 4 (over z), sub: 2 (over x), feat: 2 (over core).
Axes of the slice: x: 2, y: 2, z: 4, core: 2. Of those that a mesh axis runs over, the one named last changes fastest.
Arguments:
- vectors: bfloat16 [64, 640, 256], P(('groups', 'pairs'), 'sub'), parts along dimension 0
- affinity: bfloat16 [64, 640, 64], P(('groups', 'pairs'), 'sub', 'feat'), parts along dimension 0, may hold values from -6 to 6
- counts: int32 [64], P('groups'), parts along dimension 0, may hold values from 1 to 640, 15360 in all
- owner_map: int32 [64], P('groups'), parts along dimension 0, may hold values from 0 to 31, as said below
- pair_table: int32 [24, 2], P(('groups', 'pairs')), parts along dimension 0, may hold values from -1 to 31, as said below
Outputs:
- smoothed: bfloat16 [64, 640, 64], P(('groups', 'pairs'), 'sub', 'feat'), parts along dimension 0
There are 2 independent parts, one for each index of `groups`. A program takes and returns all parts, laid end to end along the dimension named above; each array names one. Nothing has to cross between parts.
Inputs may be any that keep to these rules, and one draw needn't show every extreme that they name: A permutation: block b is stored at position owner_map[b], which lies on index owner_map[b] // 8 of pairs. `pair_table`: index p of pairs holds rows p * 3 to (p + 1) * 3 - 1. A live row (a, b) names two different blocks and a is stored on that same device; live rows come first, the others are (-1, -1). No unordered pair is listed twice. The b blocks of one device's live rows are stored on different devices, none of them the device itself. A device holds 0 to 3 live rows; some device holds exactly 3 and some none.
All inputs are finite; a program needn't handle non-finite values.
Results may differ from a plain program's by a relative error of at most 0.0025.
Values may be sent and summed in bfloat16 or wider, within the bound.
A program may use at most 64 MiB of HBM per device.

v0:
```python
import jax
import jax.numpy as jnp
from jax import lax
from jax.sharding import PartitionSpec as P

sharpness = 8.0


def on_device(vectors, affinity, counts, owner_map, pair_table):
    pair_count = lax.axis_size("pairs")
    sub_count = lax.axis_size("sub")
    pair_index = lax.axis_index("pairs")
    sub_index = lax.axis_index("sub")
    blocks, slice_rows, emb_width = vectors.shape
    aff_cols = affinity.shape[2]
    full_rows = slice_rows * sub_count
    slot_count = pair_table.shape[0]
    block_count = counts.shape[0]
    floats = vectors.astype(jnp.float32)
    unit_rows = (
        floats * lax.rsqrt(jnp.sum(floats * floats, axis=2, keepdims=True) + 1e-06)
    ).astype(jnp.bfloat16)
    block_iota = jnp.arange(block_count, dtype=jnp.int32)
    local_iota = jnp.arange(blocks, dtype=jnp.int32)
    peer_iota = jnp.arange(pair_count, dtype=jnp.int32)
    own_slots = pair_index * blocks + local_iota
    own_counts = jnp.sum(
        jnp.where(owner_map[None, :] == own_slots[:, None], counts[None, :], 0), axis=1
    )
    first_ids = pair_table[:, 0]
    second_ids = pair_table[:, 1]
    is_live = second_ids >= 0
    first_hit = first_ids[:, None] == block_iota[None, :]
    second_hit = second_ids[:, None] == block_iota[None, :]
    first_slot = jnp.sum(jnp.where(first_hit, owner_map[None, :], 0), axis=1)
    second_slot = jnp.sum(jnp.where(second_hit, owner_map[None, :], 0), axis=1)
    second_count = jnp.sum(jnp.where(second_hit, counts[None, :], 0), axis=1)
    first_local = first_slot % blocks
    first_count = jnp.sum(
        jnp.where(first_local[:, None] == local_iota[None, :], own_counts[None, :], 0), axis=1
    )
    second_owner = second_slot // blocks
    second_local = second_slot % blocks
    wanted = (
        jnp.sum(
            jnp.where(
                is_live[:, None] & (second_owner[:, None] == peer_iota[None, :]),
                second_local[:, None] + 1,
                0,
            ),
            axis=0,
        )
        - 1
    )
    asked = lax.all_to_all(wanted[:, None], "pairs", split_axis=0, concat_axis=0, tiled=True)[:, 0]
    picked = jnp.maximum(asked, 0)
    own_units, own_aff = (
        lax.all_gather(unit_rows, "sub", axis=1, tiled=True),
        lax.all_gather(affinity, "sub", axis=1, tiled=True),
    )
    owner_safe = jnp.where(is_live, second_owner, 0)
    got_units, got_aff = (
        lax.all_to_all(
            jnp.take(unit_rows, picked, axis=0), "pairs", split_axis=0, concat_axis=0, tiled=True
        ),
        lax.all_to_all(
            jnp.take(affinity, picked, axis=0), "pairs", split_axis=0, concat_axis=0, tiled=True
        ),
    )
    far_units = jnp.take(got_units, owner_safe, axis=0)
    far_aff = jnp.take(got_aff, owner_safe, axis=0)
    row_global = sub_index * slice_rows + jnp.arange(slice_rows, dtype=jnp.int32)
    col_iota = jnp.arange(full_rows, dtype=jnp.int32)
    inputs_all = (
        far_units.reshape(slot_count, 1, slice_rows, emb_width),
        far_aff.reshape(slot_count, 1, slice_rows, aff_cols),
        first_local.reshape(slot_count, 1),
        is_live.reshape(slot_count, 1),
        first_count.reshape(slot_count, 1),
        second_count.reshape(slot_count, 1),
    )

    def tile_step(totals, inputs):
        acc_num, acc_den = totals
        b_units, b_aff, a_local, live_slot, a_count, b_count = inputs
        a_units = jnp.take(own_units, a_local, axis=0)
        a_aff = jnp.take(own_aff, a_local, axis=0)
        cosine = jnp.einsum("krd,kcd->krc", b_units, a_units, preferred_element_type=jnp.float32)
        keep_mask = (
            live_slot[:, None, None]
            & (row_global[None, :, None] < b_count[:, None, None])
            & (col_iota[None, None, :] < a_count[:, None, None])
        )
        kernel = jnp.where(keep_mask, jnp.exp(sharpness * (cosine - 1.0)), 0.0)
        rounded = kernel.astype(jnp.bfloat16)
        near_num = jnp.einsum("krc,kce->kre", rounded, a_aff, preferred_element_type=jnp.float32)
        near_den = jnp.sum(kernel, axis=2)
        back_num = jnp.einsum("krc,kre->kce", rounded, b_aff, preferred_element_type=jnp.float32)
        back_den = jnp.sum(kernel, axis=1)
        select = (a_local[:, None] == local_iota[None, :]).astype(jnp.float32)
        acc_num = acc_num + jnp.einsum(
            "kl,kce->lce", select, back_num, precision=lax.Precision.HIGHEST
        )
        acc_den = acc_den + jnp.einsum(
            "kl,kc->lc", select, back_den, precision=lax.Precision.HIGHEST
        )
        return ((acc_num, acc_den), (near_num, near_den))

    start_totals = (
        jnp.zeros((blocks, full_rows, aff_cols), jnp.float32),
        jnp.zeros((blocks, full_rows), jnp.float32),
    )
    (acc_num, acc_den), (near_num, near_den) = lax.scan(tile_step, start_totals, inputs_all)
    near_num = near_num.reshape(slot_count, slice_rows, aff_cols)
    near_den = near_den.reshape(slot_count, slice_rows)
    routing = (is_live[:, None] & (second_owner[:, None] == peer_iota[None, :])).astype(jnp.float32)
    send_num = jnp.einsum("kn,kre->nre", routing, near_num, precision=lax.Precision.HIGHEST)
    send_den = jnp.einsum("kn,kr->nr", routing, near_den, precision=lax.Precision.HIGHEST)
    came_num, came_den = (
        lax.all_to_all(
            send_num.astype(jnp.bfloat16), "pairs", split_axis=0, concat_axis=0, tiled=True
        ).astype(send_num.dtype),
        lax.all_to_all(
            send_den.astype(jnp.bfloat16), "pairs", split_axis=0, concat_axis=0, tiled=True
        ).astype(send_den.dtype),
    )
    placing = (asked[:, None] == local_iota[None, :]).astype(jnp.float32)
    far_num = jnp.einsum("nl,nre->lre", placing, came_num, precision=lax.Precision.HIGHEST)
    far_den = jnp.einsum("nl,nr->lr", placing, came_den, precision=lax.Precision.HIGHEST)
    own_num, own_den = (
        lax.psum_scatter(
            acc_num.astype(jnp.bfloat16), "sub", scatter_dimension=1, tiled=True
        ).astype(jnp.float32),
        lax.psum_scatter(
            acc_den.astype(jnp.bfloat16), "sub", scatter_dimension=1, tiled=True
        ).astype(jnp.float32),
    )
    total_num = affinity.astype(jnp.float32) + own_num + far_num
    total_den = 1.0 + own_den + far_den
    live_rows = row_global[None, :] < own_counts[:, None]
    return jnp.where(live_rows[..., None], total_num / total_den[..., None], 0.0).astype(
        jnp.bfloat16
    )


def solution(mesh):
    in_specs = (
        P(("groups", "pairs"), "sub", None),
        P(("groups", "pairs"), "sub", "feat"),
        P("groups"),
        P("groups"),
        P(("groups", "pairs"), None),
    )
    out_specs = P(("groups", "pairs"), "sub", "feat")
    return jax.shard_map(
        on_device, mesh=mesh, in_specs=in_specs, out_specs=out_specs, check_vma=False
    )
```

profile of v0, /device:TPU:0, one launch (start us, length us, event | category | flops | bytes accessed | tf_op | source)
XLA Modules:
  0.0 150.7 jit_solution(1569284218905631338)
XLA Ops:
  6.6 1.9 %fusion.29 = f32[8,320]{1,0:T(8,128)S(1)} fusion(bf16[8,320,256]{2,1,0:T(8,128)(2,1)} %param.7), kind=kLoop, calls=%fused_computation.46 | loop fusion | flops 1963520 | bytes 1320960 | tf_op jit(solution)/shard_map/reduce_sum | solution.py:21
  8.5 2.8 %fusion.30 = bf16[8,320,256]{2,1,0:T(8,128)(2,1)} fusion(bf16[8,320,256]{2,1,0:T(8,128)(2,1)} %param.7, f32[8,320]{1,0:T(8,128)S(1)} %add_rsqrt_fusion), kind=kLoop, calls=%fused_computation.47 | loop fusion | flops 1966080 | bytes 2631680 | tf_op jit(solution)/shard_map/convert_element_type | solution.py:22
  12.4 6.3 %all-to-all-start = ((s32[4,1,1]{2,1,0:T(1,128)}), s32[4,1,1]{2,1,0:T(1,128)S(1)}, u32[]{:S(2)}, u32[]{:S(2)}) async-start(s32[4,1,1]{2,1,0:T(1,128)} %copy.49), calls=%async_computation | async-start | bytes 4096 | tf_op jit(solution)/shard_map/all_to_all | solution.py:55
  19.9 4.3 %all-to-all-done = s32[4,1,1]{2,1,0:T(1,128)S(1)} async-done(((s32[4,1,1]{2,1,0:T(1,128)}), s32[4,1,1]{2,1,0:T(1,128)S(1)}, u32[]{:S(2)}, u32[]{:S(2)}) %all-to-all-start) | async-done | bytes 48 | tf_op jit(solution)/shard_map/all_to_all | solution.py:55
  25.0 1.9 %gather_fusion = bf16[4,320,256]{2,1,0:T(8,128)(2,1)S(1)} fusion(bf16[8,320,256]{2,1,0:T(8,128)(2,1)} %fusion.30, s32[1024]{0:T(1024)S(1)} %pad_clamp_fusion.1), kind=kCustom, calls=%fused_computation | custom fusion | bytes 1310736 | tf_op jit(solution)/shard_map/jit(_take)/gather | solution.py:64
  27.7 3.3 %all-to-all-start.2 = ((bf16[4,320,32]{1,2,0:T(8,128)(2,1)}), bf16[4,320,32]{1,2,0:T(8,128)(2,1)S(1)}, u32[]{:S(2)}, u32[]{:S(2)}) async-start(bf16[4,320,32]{1,2,0:T(8,128)(2,1)} %broadcast_select_fusion.1), calls=%async_computation.2 | async-start | bytes 196608 | tf_op jit(solution)/shard_map/all_to_all | solution.py:66
  32.0 4.8 %all-to-all-done.2 = bf16[4,320,32]{1,2,0:T(8,128)(2,1)S(1)} async-done(((bf16[4,320,32]{1,2,0:T(8,128)(2,1)}), bf16[4,320,32]{1,2,0:T(8,128)(2,1)S(1)}, u32[]{:S(2)}, u32[]{:S(2)}) %all-to-all-start.2) | async-done | bytes 81952 | tf_op jit(solution)/shard_map/all_to_all | solution.py:66
  36.8 3.5 %all-to-all-start.1 = ((bf16[4,320,256]{2,1,0:T(8,128)(2,1)}), bf16[4,320,256]{2,1,0:T(8,128)(2,1)S(1)}, u32[]{:S(2)}, u32[]{:S(2)}) async-start(bf16[4,320,256]{2,1,0:T(8,128)(2,1)} %broadcast_select_fusion), calls=%async_computation.1 | async-start | bytes 1310720 | tf_op jit(solution)/shard_map/all_to_all | solution.py:63
  40.3 26.8 %all_gather.7 = bf16[8,640,32]{2,1,0:T(8,128)(2,1)} all-gather(bf16[8,320,32]{2,1,0:T(8,128)(2,1)} %copy.50), channel_id=1, replica_groups=mesh['groups'=2,'pairs'=4,'sub'=2,'feat'=2] {'sub'}, dimensions={1}, use_global_device_ids=true | all-gather | bytes 491520 | tf_op jit(solution)/shard_map/all_gather | solution.py:59
  69.5 1.9 %fusion.35 = bf16[3,1,320,256]{3,2,1,0:T(8,128)(2,1)} fusion(bf16[3,320,256]{2,1,0:T(8,128)(2,1)} %gather_fusion.1, pred[3]{0:T(512)(128)(4,1)S(1)} %get-tuple-element.388), kind=kLoop, calls=%fused_computation.58 | loop fusion | flops 245760 | bytes 983043
  71.5 32.7 %while.21 = (s32[]{:T(128)}, f32[8,640,32]{2,1,0:T(8,128)S(1)}, f32[8,640]{1,0:T(8,128)S(1)}, f32[3,1,320,32]{2,3,1,0:T(8,128)}, f32[3,1,320]{2,0,1:T(4,128)S(1)...) while((s32[]{:T(128)}, f32[8,640,32]{2,1,0:T(8,128)S(1)}, ...), condition=%wide.region_10.11_spmd.clone, body=%wide.region_7.10_spmd.clone.sunk | while | flops 133197464 | bytes 3489310 | solution.py:113
  77.8 1.6 %fusion.70 = (f32[320]{0:T(512)S(1)}, f32[640]{0:T(1024)S(1)}, bf16[320,640]{1,0:T(8,128)(2,1)S(1)}) fusion(bf16[8,640,256]{2,1,0:T(8,128)(2,1)} %get-tuple-element.545, s32[]{:T(128)} %bitcast.112, pred[]{:T(512)} %bitcast.113, bf16[3,1,320,256]{3,2,1,0:T(8,128)(2,1)} %get-tuple-element.544, s32[]{:T(128)S(6)} %copy.89, ...), kind=kOutput, calls=%fused_computation.116.clone.1 | convolution fusion | flops 106454080 | bytes 906948 | tf_op jit(solution)/shard_map/while/body/eval_jaxpr/krd,kcd->krc/dot_general | solution.py:88
  79.6 1.8 %fusion.72 = f32[3,1,320,32]{2,3,1,0:T(8,128)} fusion(f32[3,1,320,32]{2,3,1,0:T(8,128)} %get-tuple-element.519, s32[]{:T(128)S(6)} %copy.89, bf16[320,640]{1,0:T(8,128)(2,1)S(1)} %get-tuple-element.494, bf16[8,640,32]{2,1,0:T(8,128)(2,1)} %get-tuple-element.547, s32[]{:T(128)} %bitcast.112, pred[]{:T(512)} %bitcast.113), kind=kOutput, calls=%fused_computation.13.clone.1 | convolution fusion | flops 13127680 | bytes 623620 | tf_op jit(solution)/shard_map/while/body/eval_jaxpr/krc,kce->kre/dot_general | solution.py:96
  88.7 1.6 %fusion.70 = (f32[320]{0:T(512)S(1)}, f32[640]{0:T(1024)S(1)}, bf16[320,640]{1,0:T(8,128)(2,1)S(1)}) fusion(bf16[8,640,256]{2,1,0:T(8,128)(2,1)} %get-tuple-element.545, s32[]{:T(128)} %bitcast.112, pred[]{:T(512)} %bitcast.113, bf16[3,1,320,256]{3,2,1,0:T(8,128)(2,1)} %get-tuple-element.544, s32[]{:T(128)S(6)} %copy.89, ...), kind=kOutput, calls=%fused_computation.116.clone.1 | convolution fusion | flops 106454080 | bytes 906948 | tf_op jit(solution)/shard_map/while/body/eval_jaxpr/krd,kcd->krc/dot_general | solution.py:88
  90.5 1.8 %fusion.72 = f32[3,1,320,32]{2,3,1,0:T(8,128)} fusion(f32[3,1,320,32]{2,3,1,0:T(8,128)} %get-tuple-element.519, s32[]{:T(128)S(6)} %copy.89, bf16[320,640]{1,0:T(8,128)(2,1)S(1)} %get-tuple-element.494, bf16[8,640,32]{2,1,0:T(8,128)(2,1)} %get-tuple-element.547, s32[]{:T(128)} %bitcast.112, pred[]{:T(512)} %bitcast.113), kind=kOutput, calls=%fused_computation.13.clone.1 | convolution fusion | flops 13127680 | bytes 623620 | tf_op jit(solution)/shard_map/while/body/eval_jaxpr/krc,kce->kre/dot_general | solution.py:96
  99.7 1.6 %fusion.70 = (f32[320]{0:T(512)S(1)}, f32[640]{0:T(1024)S(1)}, bf16[320,640]{1,0:T(8,128)(2,1)S(1)}) fusion(bf16[8,640,256]{2,1,0:T(8,128)(2,1)} %get-tuple-element.545, s32[]{:T(128)} %bitcast.112, pred[]{:T(512)} %bitcast.113, bf16[3,1,320,256]{3,2,1,0:T(8,128)(2,1)} %get-tuple-element.544, s32[]{:T(128)S(6)} %copy.89, ...), kind=kOutput, calls=%fused_computation.116.clone.1 | convolution fusion | flops 106454080 | bytes 906948 | tf_op jit(solution)/shard_map/while/body/eval_jaxpr/krd,kcd->krc/dot_general | solution.py:88
  101.4 1.8 %fusion.72 = f32[3,1,320,32]{2,3,1,0:T(8,128)} fusion(f32[3,1,320,32]{2,3,1,0:T(8,128)} %get-tuple-element.519, s32[]{:T(128)S(6)} %copy.89, bf16[320,640]{1,0:T(8,128)(2,1)S(1)} %get-tuple-element.494, bf16[8,640,32]{2,1,0:T(8,128)(2,1)} %get-tuple-element.547, s32[]{:T(128)} %bitcast.112, pred[]{:T(512)} %bitcast.113), kind=kOutput, calls=%fused_computation.13.clone.1 | convolution fusion | flops 13127680 | bytes 623620 | tf_op jit(solution)/shard_map/while/body/eval_jaxpr/krc,kce->kre/dot_general | solution.py:96
  106.4 4.5 %copy.61 = bf16[8,640,32]{0,2,1:T(8,128)(2,1)} copy(bf16[8,640,32]{1,0,2:T(8,128)(2,1)S(1)} %copy.54) | data formatting | bytes 655360
  110.9 9.0 %reshape.432 = bf16[640,256]{1,0:T(8,128)(2,1)} reshape(bf16[640,32,8]{2,1,0:T(8,128)(2,1)} %bitcast.118) | data formatting | bytes 655360
  121.9 4.6 %all-to-all-start.4 = ((bf16[4,2,160]{2,1,0:T(2,128)(2,1)}), bf16[4,2,160]{2,1,0:T(2,128)(2,1)S(1)}, u32[]{:S(2)}, u32[]{:S(2)}) async-start(bf16[4,2,160]{2,1,0:T(2,128)(2,1)} %reshape.438), calls=%async_computation.4 | async-start | bytes 8192 | tf_op jit(solution)/shard_map/all_to_all | solution.py:123
  127.5 4.5 %all-to-all-done.4 = bf16[4,2,160]{2,1,0:T(2,128)(2,1)S(1)} async-done(((bf16[4,2,160]{2,1,0:T(2,128)(2,1)}), bf16[4,2,160]{2,1,0:T(2,128)(2,1)S(1)}, u32[]{:S(2)}, u32[]{:S(2)}) %all-to-all-start.4) | async-done | bytes 2592 | tf_op jit(solution)/shard_map/all_to_all | solution.py:123
  132.1 3.3 %all-to-all-start.3 = ((bf16[4,320,32]{1,2,0:T(8,128)(2,1)}), bf16[4,320,32]{1,2,0:T(8,128)(2,1)S(1)}, u32[]{:S(2)}, u32[]{:S(2)}) async-start(bf16[4,320,32]{1,2,0:T(8,128)(2,1)} %copy.56), calls=%async_computation.3 | async-start | bytes 196608 | tf_op jit(solution)/shard_map/all_to_all | solution.py:120
  136.7 4.1 %reshape.433 = bf16[320,32,8]{2,1,0:T(8,128)(2,1)S(1)} reshape(bf16[320,256]{1,0:T(8,128)(2,1)} %reduce-scatter.7.cloned.1.call-done) | data formatting | bytes 327680
  140.8 2.3 %copy.62 = bf16[8,320,32]{1,0,2:T(8,128)(2,1)S(1)} copy(bf16[8,320,32]{0,2,1:T(8,128)(2,1)S(1)} %bitcast.119) | data formatting | bytes 327680
  (100 shorter events, 31.3 us)
Async XLA Ops:
  6.5 4.8 %copy-start.3 = (s32[3,2]{0,1:T(2,128)S(1)}, s32[3,2]{0,1:T(2,128)}, u32[]{:S(2)}) copy-start(s32[3,2]{0,1:T(2,128)} %param.11) | copy-start | bytes 76
  6.5 4.8 %copy-start.4 = (s32[32]{0:T(128)S(1)}, s32[32]{0:T(128)}, u32[]{:S(2)}) copy-start(s32[32]{0:T(128)} %param.10) | copy-start | bytes 388
  6.5 4.8 %copy-start.5 = (s32[32]{0:T(128)S(1)}, s32[32]{0:T(128)}, u32[]{:S(2)}) copy-start(s32[32]{0:T(128)} %param.9) | copy-start | bytes 388
  6.5 12.2 %copy-start = (bf16[8,320,32]{1,2,0:T(8,128)(2,1)S(1)}, bf16[8,320,32]{1,2,0:T(8,128)(2,1)}, u32[]{:S(2)}) copy-start(bf16[8,320,32]{1,2,0:T(8,128)(2,1)} %param.8) | copy-start | bytes 491524
  6.5 64.9 %all-gather.2.cloned.1.call-start = ((), (), s32[]{:S(2)}) async-start(), calls=%async_computation.7 | async-start | bytes 3932160 | tf_op jit(solution)/shard_map/all_gather | solution.py:58
  12.4 11.8 %all-to-all-start = ((s32[4,1,1]{2,1,0:T(1,128)}), s32[4,1,1]{2,1,0:T(1,128)S(1)}, u32[]{:S(2)}, u32[]{:S(2)}) async-start(s32[4,1,1]{2,1,0:T(1,128)} %copy.49), calls=%async_computation | async-start | bytes 4096 | tf_op jit(solution)/shard_map/all_to_all | solution.py:55
  27.7 9.1 %all-to-all-start.2 = ((bf16[4,320,32]{1,2,0:T(8,128)(2,1)}), bf16[4,320,32]{1,2,0:T(8,128)(2,1)S(1)}, u32[]{:S(2)}, u32[]{:S(2)}) async-start(bf16[4,320,32]{1,2,0:T(8,128)(2,1)} %broadcast_select_fusion.1), calls=%async_computation.2 | async-start | bytes 196608 | tf_op jit(solution)/shard_map/all_to_all | solution.py:66
  36.8 31.4 %all-to-all-start.1 = ((bf16[4,320,256]{2,1,0:T(8,128)(2,1)}), bf16[4,320,256]{2,1,0:T(8,128)(2,1)S(1)}, u32[]{:S(2)}, u32[]{:S(2)}) async-start(bf16[4,320,256]{2,1,0:T(8,128)(2,1)} %broadcast_select_fusion), calls=%async_computation.1 | async-start | bytes 1310720 | tf_op jit(solution)/shard_map/all_to_all | solution.py:63
  40.3 95.2 %reduce-scatter.9.cloned.1.call-start = ((), (), s32[]{:S(2)}) async-start(), calls=%async_computation.9 | async-start | bytes 245760
  105.0 31.6 %reduce-scatter.7.cloned.1.call-start = ((), (), s32[]{:S(2)}) async-start(), calls=%async_computation.8 | async-start | bytes 491520
  110.9 15.6 %copy-start.2 = (f32[3,1,320,32]{2,3,1,0:T(8,128)S(1)}, f32[3,1,320,32]{2,3,1,0:T(8,128)}, u32[]{:S(2)}) copy-start(f32[3,1,320,32]{2,3,1,0:T(8,128)} %get-tuple-element.206) | copy-start | bytes 368644
  121.9 10.2 %all-to-all-start.4 = ((bf16[4,2,160]{2,1,0:T(2,128)(2,1)}), bf16[4,2,160]{2,1,0:T(2,128)(2,1)S(1)}, u32[]{:S(2)}, u32[]{:S(2)}) async-start(bf16[4,2,160]{2,1,0:T(2,128)(2,1)} %reshape.438), calls=%async_computation.4 | async-start | bytes 8192 | tf_op jit(solution)/shard_map/all_to_all | solution.py:123
  132.1 11.0 %all-to-all-start.3 = ((bf16[4,320,32]{1,2,0:T(8,128)(2,1)}), bf16[4,320,32]{1,2,0:T(8,128)(2,1)S(1)}, u32[]{:S(2)}, u32[]{:S(2)}) async-start(bf16[4,320,32]{1,2,0:T(8,128)(2,1)} %copy.56), calls=%async_computation.3 | async-start | bytes 196608 | tf_op jit(solution)/shard_map/all_to_all | solution.py:120
  136.7 6.4 %copy-start.1 = (bf16[8,320,32]{1,2,0:T(8,128)(2,1)S(1)}, bf16[8,320,32]{1,2,0:T(8,128)(2,1)}, u32[]{:S(2)}) copy-start(bf16[8,320,32]{1,2,0:T(8,128)(2,1)} %param.8) | copy-start | bytes 491524
Sparse Core Ops, SparseCore 0:
  11.5 49.6 all-gather.1
  105.2 10.5 reduce-scatter.8
  120.0 12.4 reduce-scatter.6
where the time goes:
time: 152 us; the launch traced here: 151 us
  local copies, waits for them, and re-layouts  37.5 us (25%)
  blocking collectives  26.8 us (18%)
  starting transfers between devices  21.1 us (14%)
  other arithmetic  20 us (13%)
  waiting for transfers between devices  13.8 us (9%)
  between operations  13.3 us (9%)
  matrix products  12.2 us (8%)
  loops' own time  6.01 us (4%)
    all_gather x1, blocking collectives, on_device(): lax.all_gather(affinity, 'sub', axis=1, tiled=True)  26.8 us
    unnamed x21, local copies, waits for them, and re-layouts  23.6 us
    all_to_all x1, starting transfers between devices, on_device(): lax.all_to_all(wanted[:, None], 'pairs', split_axis=0, concat_axis=0, til...  6.32 us
    another operation x1, loops' own time, on_device(): lax.scan(tile_step, start_totals, inputs_all)  6.01 us
    dynamic_slice x9, local copies, waits for them, and re-layouts, on_device(): lax.scan(tile_step, start_totals, inputs_all)  5.54 us
    dot_general x3, matrix products, tile_step(): jnp.einsum('krc,kce->kre', rounded, a_aff, preferred_element_type=jnp.flo...  5.34 us
    all_to_all x1, waiting for transfers between devices, on_device(): lax.all_to_all(jnp.take(affinity, picked, axis=0), 'pairs', split_axis=0,...  4.83 us
    dot_general x3, matrix products, tile_step(): jnp.einsum('krd,kcd->krc', b_units, a_units, preferred_element_type=jnp.f...  4.79 us
  transfers between devices with their start and end apart: 8, of which 3 were waited for; matrix products, arithmetic and copies ran while one was open for 24% of the time, Pallas kernels for 0%

commit v1 on v0

v1 whole, which is shorter than its diff:
```python
import functools

import jax
import jax.numpy as jnp
from jax import lax
from jax.experimental import pallas as pl
from jax.experimental.pallas import tpu as pltpu
from jax.sharding import PartitionSpec as P

sharpness = 8.0
MESH = pl.DeviceIdType.MESH


def loop(count, body, unrolled=4):
    if count <= unrolled:
        for i in range(count):
            body(i)
    else:

        def step(i, carry):
            body(i)
            return carry

        lax.fori_loop(0, count, step, 0)


def fold(count, body, start, unrolled=4):
    if count <= unrolled:
        for i in range(count):
            start = body(i, start)
        return start
    return lax.fori_loop(0, count, body, start)


def kernel(
    pair_count,
    sub_count,
    vec_ref,
    aff_ref,
    counts_ref,
    owner_ref,
    table_ref,
    table_vec_ref,
    out_ref,
    own_units,
    own_aug,
    far_units,
    far_aug,
    send_units,
    send_aug,
    got_units,
    got_aug,
    near_send,
    near_got,
    back_own,
    back_send,
    back_got,
    tables_vec,
    tables,
    tab_send_sem,
    tab_got_sem,
    tab_local_sem,
    sub_send_sem,
    sub_got_sem,
    pair_send_sem,
    pair_got_sem,
    near_send_sem,
    near_got_sem,
    back_send_sem,
    back_got_sem,
):
    me = lax.axis_index("pairs")
    sub = lax.axis_index("sub")
    blocks, rows, _ = vec_ref.shape
    cols = aff_ref.shape[1]
    height = own_aug.shape[1]
    slots = table_ref.shape[1]
    peers = pair_count - 1
    others = sub_count - 1

    def peer_of(e):
        return lax.rem(me + e + 1, pair_count)

    def sub_of(u):
        return lax.rem(sub + u + 1, sub_count)

    def place(block):
        return owner_ref[jnp.maximum(block, 0)]

    def find(entry, target):
        def step(k, found):
            first, second = entry(0, k), entry(1, k)
            hit = (second >= 0) & (lax.div(place(second), jnp.int32(blocks)) == target)
            return jnp.where(hit, first, found[0]), jnp.where(hit, second, found[1])

        return fold(slots, step, (jnp.int32(-1), jnp.int32(-1)))

    def local_of(block):
        return lax.rem(place(block), jnp.int32(blocks))

    def own_pair(e):
        return find(lambda i, k: table_ref[i, k], peer_of(e))

    def asked_pair(e):
        return find(lambda i, k: tables[e, i, k], me)

    def fill(block, units_ref, aug_ref, e):
        floats = vec_ref[block].astype(jnp.float32)
        scale = lax.rsqrt(jnp.sum(floats * floats, axis=1, keepdims=True) + 1e-06)
        units_ref[e] = (floats * scale).astype(jnp.bfloat16)
        aug_ref[e, 0:cols, :] = aff_ref[block]
        aug_ref[e, cols:height, :] = jnp.ones((height - cols, rows), jnp.bfloat16)

    def remote(src, dst, send_sem, got_sem, device):
        return pltpu.make_async_remote_copy(
            src_ref=src,
            dst_ref=dst,
            send_sem=send_sem,
            recv_sem=got_sem,
            device_id=device,
            device_id_type=MESH,
        )

    def table_copy(e):
        there = peers - 1 - e
        return remote(
            table_vec_ref,
            tables_vec.at[there],
            tab_send_sem.at[e],
            tab_got_sem.at[there],
            {"pairs": peer_of(e)},
        )

    def sub_copies(e, u):
        there = others - 1 - u
        to = {"sub": sub_of(u)}
        return (
            remote(
                own_units.at[e],
                far_units.at[there, e],
                sub_send_sem.at[0, u, e],
                sub_got_sem.at[0, there, e],
                to,
            ),
            remote(
                own_aug.at[e],
                far_aug.at[there, e],
                sub_send_sem.at[1, u, e],
                sub_got_sem.at[1, there, e],
                to,
            ),
        )

    def pair_copies(e):
        there = peers - 1 - e
        to = {"pairs": peer_of(e)}
        return (
            remote(
                send_units.at[e],
                got_units.at[there],
                pair_send_sem.at[0, e],
                pair_got_sem.at[0, there],
                to,
            ),
            remote(
                send_aug.at[e],
                got_aug.at[there],
                pair_send_sem.at[1, e],
                pair_got_sem.at[1, there],
                to,
            ),
        )

    def near_copy(e):
        there = peers - 1 - e
        return remote(
            near_send.at[e],
            near_got.at[there],
            near_send_sem.at[e],
            near_got_sem.at[there],
            {"pairs": peer_of(e)},
        )

    def back_copy(e, u):
        there = others - 1 - u
        return remote(
            back_send.at[u, e],
            back_got.at[there, e],
            back_send_sem.at[u, e],
            back_got_sem.at[there, e],
            {"sub": sub_of(u)},
        )

    barrier = pltpu.get_barrier_semaphore()

    def greet_peer(e):
        pl.semaphore_signal(barrier, inc=1, device_id={"pairs": peer_of(e)}, device_id_type=MESH)

    def greet_sub(u):
        pl.semaphore_signal(barrier, inc=1, device_id={"sub": sub_of(u)}, device_id_type=MESH)

    loop(peers, greet_peer)
    loop(others, greet_sub)
    pl.semaphore_wait(barrier, peers + others)

    loop(peers, lambda e: table_copy(e).start())

    def start_own(e):
        fill(local_of(own_pair(e)[0]), own_units, own_aug, e)

        def send(u):
            for copy in sub_copies(e, u):
                copy.start()

        loop(others, send)

    loop(peers, start_own)

    def table_in(e):
        table_copy(peers - 1 - e).wait_recv()

    loop(peers, table_in)
    to_scalars = pltpu.make_async_copy(tables_vec, tables, tab_local_sem)
    to_scalars.start()
    to_scalars.wait()

    def start_pair(e):
        fill(local_of(asked_pair(e)[1]), send_units, send_aug, e)
        for copy in pair_copies(e):
            copy.start()

    loop(peers, start_pair)

    lane = lax.broadcasted_iota(jnp.int32, (height, rows), 1)

    def cut(aug, first_row, count):
        keep = first_row + lane < count
        return jnp.where(keep, aug.astype(jnp.float32), 0.0).astype(jnp.bfloat16)

    def tile(a_units, a_aug, b_units, b_aug):
        cosine = lax.dot_general(
            b_units, a_units, (((1,), (1,)), ((), ())), preferred_element_type=jnp.float32
        )
        rounded = jnp.exp(sharpness * (cosine - 1.0)).astype(jnp.bfloat16)
        near = lax.dot_general(
            a_aug, rounded, (((1,), (1,)), ((), ())), preferred_element_type=jnp.float32
        )
        back = jnp.dot(b_aug, rounded, preferred_element_type=jnp.float32)
        return near, back

    def pair_step(e):
        first, second = own_pair(e)
        live = second >= 0
        a_count = jnp.where(live, counts_ref[jnp.maximum(first, 0)], 0)
        b_count = jnp.where(live, counts_ref[jnp.maximum(second, 0)], 0)
        for copy in pair_copies(peers - 1 - e):
            copy.wait_recv()
        b_units = got_units[e]
        b_aug = cut(got_aug[e], sub * rows, b_count)
        near, back = tile(own_units[e], cut(own_aug[e], sub * rows, a_count), b_units, b_aug)
        back_own[e] = back
        for u in range(others):
            for copy in sub_copies(e, others - 1 - u):
                copy.wait_recv()
            more, back = tile(
                far_units[u, e], cut(far_aug[u, e], sub_of(u) * rows, a_count), b_units, b_aug
            )
            near = near + more
            back_send[u, e] = back.astype(jnp.bfloat16)
            back_copy(e, u).start()
        near_send[e] = near.astype(jnp.bfloat16)
        near_copy(e).start()

    loop(peers, pair_step)

    def count_step(b, found):
        at = owner_ref[b] - me * blocks
        return tuple(jnp.where(at == l, counts_ref[b], found[l]) for l in range(blocks))

    own_counts = fold(
        counts_ref.shape[0], count_step, (jnp.int32(0),) * blocks, unrolled=32
    )

    def arrive(e):
        near_copy(peers - 1 - e).wait_recv()

        def back_in(u):
            back_copy(e, others - 1 - u).wait_recv()

        loop(others, back_in)

    loop(peers, arrive)

    column = lax.broadcasted_iota(jnp.int32, (cols, rows), 1)
    for l in range(blocks):

        def add(e, total, l=l):
            own, asked = own_pair(e), asked_pair(e)
            mine = (own[1] >= 0) & (local_of(own[0]) == l)
            theirs = (asked[1] >= 0) & (local_of(asked[1]) == l)
            part = back_own[e]
            for u in range(others):
                part = part + back_got[u, e].astype(jnp.float32)
            total = total + jnp.where(mine, part, 0.0)
            return total + jnp.where(theirs, near_got[e].astype(jnp.float32), 0.0)

        total = fold(peers, add, jnp.zeros((height, rows), jnp.float32))
        numer = aff_ref[l].astype(jnp.float32) + total[0:cols]
        denom = 1.0 + total[cols : cols + 1]
        keep = sub * rows + column < own_counts[l]
        out_ref[l] = jnp.where(keep, numer / denom, 0.0).astype(jnp.bfloat16)

    def sent(e):
        table_copy(e).wait_send()
        near_copy(e).wait_send()
        for copy in pair_copies(e):
            copy.wait_send()

        def sub_sent(u):
            back_copy(e, u).wait_send()
            for copy in sub_copies(e, u):
                copy.wait_send()

        loop(others, sub_sent)

    loop(peers, sent)


def on_device(vectors, affinity, counts, owner_map, pair_table):
    pair_count = lax.axis_size("pairs")
    sub_count = lax.axis_size("sub")
    blocks, rows, width = vectors.shape
    cols = affinity.shape[2]
    height = cols + 16
    peers, others = pair_count - 1, sub_count - 1
    slots = pair_table.shape[0]
    table = pair_table.T
    half = jnp.bfloat16
    dma = pltpu.SemaphoreType.DMA
    vmem = pl.BlockSpec(memory_space=pltpu.VMEM)
    smem = pl.BlockSpec(memory_space=pltpu.SMEM)
    out = pl.pallas_call(
        functools.partial(kernel, pair_count, sub_count),
        out_shape=jax.ShapeDtypeStruct((blocks, cols, rows), half),
        in_specs=[vmem, vmem, smem, smem, smem, vmem],
        out_specs=vmem,
        scratch_shapes=[
            pltpu.VMEM((peers, rows, width), half),
            pltpu.VMEM((peers, height, rows), half),
            pltpu.VMEM((others, peers, rows, width), half),
            pltpu.VMEM((others, peers, height, rows), half),
            pltpu.VMEM((peers, rows, width), half),
            pltpu.VMEM((peers, height, rows), half),
            pltpu.VMEM((peers, rows, width), half),
            pltpu.VMEM((peers, height, rows), half),
            pltpu.VMEM((peers, height, rows), half),
            pltpu.VMEM((peers, height, rows), half),
            pltpu.VMEM((peers, height, rows), jnp.float32),
            pltpu.VMEM((others, peers, height, rows), half),
            pltpu.VMEM((others, peers, height, rows), half),
            pltpu.VMEM((peers, 2, slots), jnp.int32),
            pltpu.SMEM((peers, 2, slots), jnp.int32),
            dma((peers,)),
            dma((peers,)),
            dma(()),
            dma((2, others, peers)),
            dma((2, others, peers)),
            dma((2, peers)),
            dma((2, peers)),
            dma((peers,)),
            dma((peers,)),
            dma((others, peers)),
            dma((others, peers)),
        ],
        compiler_params=pltpu.CompilerParams(
            collective_id=0, has_side_effects=True, vmem_limit_bytes=50 * 1024 * 1024
        ),
        name="pair_sums",
    )(vectors, affinity.transpose(0, 2, 1), counts, owner_map, table, table)
    return out.transpose(0, 2, 1)


def solution(mesh):
    in_specs = (
        P(("groups", "pairs"), "sub", None),
        P(("groups", "pairs"), "sub", "feat"),
        P("groups"),
        P("groups"),
        P(("groups", "pairs"), None),
    )
    out_specs = P(("groups", "pairs"), "sub", "feat")
    return jax.shard_map(
        on_device, mesh=mesh, in_specs=in_specs, out_specs=out_specs, check_vma=False
    )
```

time: 152 us -> 41.4 us (0.27)
  Pallas kernels: 0 us -> 36.3 us
  local copies, waits for them, and re-layouts: 37.5 us -> 4.91 us
  blocking collectives: 26.8 us -> 0 us
  starting transfers between devices: 21.1 us -> 0 us
  other arithmetic: 20 us -> 0 us
  waiting for transfers between devices: 13.8 us -> 0 us
  between operations: 13.3 us -> 0.01 us
  matrix products: 12.2 us -> 0 us
  loops' own time: 6.01 us -> 0 us
    pallas_call x0 -> x1, Pallas kernels: none -> 36.3 us  [on_device(): pl.pallas_call(functools.partial(kernel, pair_count, sub_count), out_shap...]
    all_gather x1 -> x0, blocking collectives: 26.8 us -> none  [on_device(): lax.all_gather(affinity, 'sub', axis=1, tiled=True)]
    all_to_all x5 -> x0, starting transfers between devices: 21 us -> none  [the longest x1 6.32 us: on_device(): lax.all_to_all(wanted[:, None], 'pairs', split_axis=0, concat_axis=0, til...]
    unnamed x21 -> x11, local copies, waits for them, and re-layouts: 23.6 us -> 4.91 us
    all_to_all x5 -> x0, waiting for transfers between devices: 13.7 us -> none  [the longest x1 4.83 us: on_device(): lax.all_to_all(jnp.take(affinity, picked, axis=0), 'pairs', split_axis=0,...]
    dot_general x13 -> x0, matrix products: 12.2 us -> none  [the longest x3 5.34 us: tile_step(): jnp.einsum('krc,kce->kre', rounded, a_aff, preferred_element_type=jnp.flo...]
    another operation x1 -> x0, loops' own time: 6.01 us -> none  [on_device(): lax.scan(tile_step, start_totals, inputs_all)]
    dynamic_slice x9 -> x0, local copies, waits for them, and re-layouts: 5.54 us -> none  [on_device(): lax.scan(tile_step, start_totals, inputs_all)]
  transfers between devices with their start and end apart: 8 -> 0, of which waited for: 3 -> 0; matrix products, arithmetic and copies ran while one was open for 24% -> 0% of each run, Pallas kernels for 0% -> 0%
where the time goes in v1:
time: 41.4 us; the launch traced here: 41.2 us
  Pallas kernels  36.3 us (88%)
  local copies, waits for them, and re-layouts  4.91 us (12%)
    pallas_call x1, Pallas kernels, on_device(): pl.pallas_call(functools.partial(kernel, pair_count, sub_count), out_shap...  36.3 us
    unnamed x11, local copies, waits for them, and re-layouts  4.91 us

profile of v1, /device:TPU:0, one launch (start us, length us, event | category | flops | bytes accessed | tf_op | source)
XLA Modules:
  0.0 41.2 jit_solution(7512335019192067110)
XLA Ops:
  0.0 0.0 copy-start
  0.0 1.3 %copy-done = bf16[8,320,256]{2,1,0:T(8,128)(2,1)S(1)} copy-done((bf16[8,320,256]{2,1,0:T(8,128)(2,1)S(1)}, bf16[8,320,256]{2,1,0:T(8,128)(2,1)}, u32[]{:S(2)}) %copy-start) | copy-done | bytes 1310744
  1.3 0.0 copy-start.1
  1.3 0.9 %copy-done.1 = bf16[8,320,32]{1,2,0:T(8,128)(2,1)S(1)} copy-done((bf16[8,320,32]{1,2,0:T(8,128)(2,1)S(1)}, bf16[8,320,32]{1,2,0:T(8,128)(2,1)}, u32[]{:S(2)}) %copy-start.1) | copy-done | bytes 163864
  2.2 0.0 copy-start.2
  2.2 0.7 %copy-done.2 = s32[3,2]{0,1:T(2,128)S(1)} copy-done((s32[3,2]{0,1:T(2,128)S(1)}, s32[3,2]{0,1:T(2,128)}, u32[]{:S(2)}) %copy-start.2) | copy-done | bytes 48
  2.9 0.0 copy-start.3
  2.9 0.7 %copy-done.3 = s32[32]{0:T(128)S(1)} copy-done((s32[32]{0:T(128)S(1)}, s32[32]{0:T(128)}, u32[]{:S(2)}) %copy-start.3) | copy-done | bytes 152
  3.6 0.0 copy-start.4
  3.6 0.7 %copy-done.4 = s32[32]{0:T(128)S(1)} copy-done((s32[32]{0:T(128)S(1)}, s32[32]{0:T(128)}, u32[]{:S(2)}) %copy-start.4) | copy-done | bytes 152
  4.2 36.3 %pair_sums.1 = bf16[8,32,320]{2,1,0:T(8,128)(2,1)S(1)} custom-call(bf16[8,320,256]{2,1,0:T(8,128)(2,1)S(1)} %copy-done, bf16[8,32,320]{2,1,0:T(8,128)(2,1)S(1)} %bitcast.4, s32[32]{0:T(128)S(1)} %copy-done.3, s32[32]{0:T(128)S(1)} %copy-done.4, s32[2,3]{1,0:T(2,128)S(1)} %bitcast.5, s32[2,3]{1,0:T(2,128)S(1)} %bitcast.6), custom_call_target="tpu_custom_call" | custom-call | tf_op jit(solution)/shard_map/pair_sums/pallas_call | solution.py:342
  40.5 0.7 %copy.7 = bf16[8,320,32]{1,2,0:T(8,128)(2,1)} copy(bf16[8,320,32]{1,2,0:T(8,128)(2,1)S(1)} %bitcast.3) | data formatting | bytes 327680
Async XLA Ops:
  0.0 1.3 %copy-start = (bf16[8,320,256]{2,1,0:T(8,128)(2,1)S(1)}, bf16[8,320,256]{2,1,0:T(8,128)(2,1)}, u32[]{:S(2)}) copy-start(bf16[8,320,256]{2,1,0:T(8,128)(2,1)} %vec_ref.1) | copy-start | bytes 3932164
  1.3 0.9 %copy-start.1 = (bf16[8,320,32]{1,2,0:T(8,128)(2,1)S(1)}, bf16[8,320,32]{1,2,0:T(8,128)(2,1)}, u32[]{:S(2)}) copy-start(bf16[8,320,32]{1,2,0:T(8,128)(2,1)} %param.6) | copy-start | bytes 491524
  2.2 0.7 %copy-start.2 = (s32[3,2]{0,1:T(2,128)S(1)}, s32[3,2]{0,1:T(2,128)}, u32[]{:S(2)}) copy-start(s32[3,2]{0,1:T(2,128)} %param.9) | copy-start | bytes 76
  2.9 0.7 %copy-start.3 = (s32[32]{0:T(128)S(1)}, s32[32]{0:T(128)}, u32[]{:S(2)}) copy-start(s32[32]{0:T(128)} %counts_ref.1) | copy-start | bytes 388
  3.6 0.7 %copy-start.4 = (s32[32]{0:T(128)S(1)}, s32[32]{0:T(128)}, u32[]{:S(2)}) copy-start(s32[32]{0:T(128)} %owner_ref.1) | copy-start | bytes 388

commit v2 on v1

--- a/solution.py
+++ b/solution.py
@@ -35,13 +35,18 @@
 def kernel(
     pair_count,
     sub_count,
+    core_count,
+    vec_hbm,
+    aff_hbm,
+    counts_hbm,
+    owner_hbm,
+    table_hbm,
+    out_ref,
     vec_ref,
     aff_ref,
     counts_ref,
     owner_ref,
     table_ref,
-    table_vec_ref,
-    out_ref,
     own_units,
     own_aug,
     far_units,
@@ -57,6 +62,7 @@
     back_got,
     tables_vec,
     tables,
+    fetch_sem,
     tab_send_sem,
     tab_got_sem,
     tab_local_sem,
@@ -68,11 +74,18 @@
     near_got_sem,
     back_send_sem,
     back_got_sem,
+    far_send_sem,
+    far_got_sem,
+    share_send_sem,
+    share_got_sem,
 ):
     me = lax.axis_index("pairs")
     sub = lax.axis_index("sub")
-    blocks, rows, _ = vec_ref.shape
+    core = lax.axis_index("feat")
+    blocks, _, part, width = vec_ref.shape
+    rows = part * core_count
     cols = aff_ref.shape[1]
+    mates = core_count - 1
     height = own_aug.shape[1]
     slots = table_ref.shape[1]
     peers = pair_count - 1
@@ -98,16 +111,36 @@
     def local_of(block):
         return lax.rem(place(block), jnp.int32(blocks))
 
+    def mate_of(v):
+        return lax.rem(core + v + 1, core_count)
+
+    known = {}
+
+    def once(name, e, work):
+        if not isinstance(e, int):
+            return work()
+        if (name, e) not in known:
+            known[name, e] = work()
+        return known[name, e]
+
     def own_pair(e):
-        return find(lambda i, k: table_ref[i, k], peer_of(e))
+        return once("own", e, lambda: find(lambda i, k: table_ref[i, k], peer_of(e)))
 
     def asked_pair(e):
-        return find(lambda i, k: tables[e, i, k], me)
-
-    def fill(block, units_ref, aug_ref, e):
-        floats = vec_ref[block].astype(jnp.float32)
+        return once("asked", e, lambda: find(lambda i, k: tables[e, i, k], me))
+
+    def own_local(e):
+        return once("own at", e, lambda: local_of(own_pair(e)[0]))
+
+    def asked_local(e):
+        return once("asked at", e, lambda: local_of(asked_pair(e)[1]))
+
+    def unit(floats):
+        floats = floats.astype(jnp.float32)
         scale = lax.rsqrt(jnp.sum(floats * floats, axis=1, keepdims=True) + 1e-06)
-        units_ref[e] = (floats * scale).astype(jnp.bfloat16)
+        return (floats * scale).astype(jnp.bfloat16)
+
+    def fill_aug(block, aug_ref, e):
         aug_ref[e, 0:cols, :] = aff_ref[block]
         aug_ref[e, cols:height, :] = jnp.ones((height - cols, rows), jnp.bfloat16)
 
@@ -124,7 +157,7 @@
     def table_copy(e):
         there = peers - 1 - e
         return remote(
-            table_vec_ref,
+            table_hbm,
             tables_vec.at[there],
             tab_send_sem.at[e],
             tab_got_sem.at[there],
@@ -136,8 +169,8 @@
         to = {"sub": sub_of(u)}
         return (
             remote(
-                own_units.at[e],
-                far_units.at[there, e],
+                own_units.at[e, core],
+                far_units.at[there, e, core],
                 sub_send_sem.at[0, u, e],
                 sub_got_sem.at[0, there, e],
                 to,
@@ -157,7 +190,7 @@
         return (
             remote(
                 send_units.at[e],
-                got_units.at[there],
+                got_units.at[there, core],
                 pair_send_sem.at[0, e],
                 pair_got_sem.at[0, there],
                 to,
@@ -171,6 +204,28 @@
             ),
         )
 
+    def far_share(e, u, v):
+        there = mates - 1 - v
+        piece = far_units.at[u, e, core]
+        return remote(
+            piece,
+            piece,
+            far_send_sem.at[u, e, v],
+            far_got_sem.at[u, e, there],
+            {"feat": mate_of(v)},
+        )
+
+    def got_share(e, v):
+        there = mates - 1 - v
+        piece = got_units.at[e, core]
+        return remote(
+            piece,
+            piece,
+            share_send_sem.at[e, v],
+            share_got_sem.at[e, there],
+            {"feat": mate_of(v)},
+        )
+
     def near_copy(e):
         there = peers - 1 - e
         return remote(
@@ -191,6 +246,21 @@
             {"sub": sub_of(u)},
         )
 
+    fetches = [
+        pltpu.make_async_copy(src, dst, fetch_sem.at[i])
+        for i, (src, dst) in enumerate(
+            [
+                (table_hbm, table_ref),
+                (owner_hbm, owner_ref),
+                (counts_hbm, counts_ref),
+                (vec_hbm, vec_ref),
+                (aff_hbm, aff_ref),
+            ]
+        )
+    ]
+    for fetch in fetches:
+        fetch.start()
+
     barrier = pltpu.get_barrier_semaphore()
 
     def greet_peer(e):
@@ -200,13 +270,22 @@
         pl.semaphore_signal(barrier, inc=1, device_id={"sub": sub_of(u)}, device_id_type=MESH)
 
     loop(peers, greet_peer)
+    def greet_mate(v):
+        pl.semaphore_signal(barrier, inc=1, device_id={"feat": mate_of(v)}, device_id_type=MESH)
+
     loop(others, greet_sub)
-    pl.semaphore_wait(barrier, peers + others)
+    loop(mates, greet_mate)
+    pl.semaphore_wait(barrier, peers + others + mates)
 
     loop(peers, lambda e: table_copy(e).start())
+    for fetch in fetches:
+        fetch.wait()
 
     def start_own(e):
-        fill(local_of(own_pair(e)[0]), own_units, own_aug, e)
+        own_units[e] = unit(vec_ref[own_local(e)].reshape(rows, width)).reshape(
+            core_count, part, width
+        )
+        fill_aug(own_local(e), own_aug, e)
 
         def send(u):
             for copy in sub_copies(e, u):
@@ -225,11 +304,36 @@
     to_scalars.wait()
 
     def start_pair(e):
-        fill(local_of(asked_pair(e)[1]), send_units, send_aug, e)
+        send_units[e] = unit(vec_ref[asked_local(e), core])
+        fill_aug(asked_local(e), send_aug, e)
         for copy in pair_copies(e):
             copy.start()
 
     loop(peers, start_pair)
+
+    def count_step(b, found):
+        at = owner_ref[b] - me * blocks
+        return tuple(jnp.where(at == l, counts_ref[b], found[l]) for l in range(blocks))
+
+    own_counts = fold(
+        counts_ref.shape[0], count_step, (jnp.int32(0),) * blocks, unrolled=32
+    )
+
+    def share_far(e):
+        for u in range(others):
+            for copy in sub_copies(e, others - 1 - u):
+                copy.wait_recv()
+            for v in range(mates):
+                far_share(e, u, v).start()
+
+    def share_got(e):
+        for copy in pair_copies(peers - 1 - e):
+            copy.wait_recv()
+        for v in range(mates):
+            got_share(e, v).start()
+
+    loop(peers, share_far)
+    loop(peers, share_got)
 
     lane = lax.broadcasted_iota(jnp.int32, (height, rows), 1)
 
@@ -253,17 +357,22 @@
         live = second >= 0
         a_count = jnp.where(live, counts_ref[jnp.maximum(first, 0)], 0)
         b_count = jnp.where(live, counts_ref[jnp.maximum(second, 0)], 0)
-        for copy in pair_copies(peers - 1 - e):
-            copy.wait_recv()
-        b_units = got_units[e]
+        for v in range(mates):
+            got_share(e, mates - 1 - v).wait_recv()
+        b_units = got_units[e].reshape(rows, width)
         b_aug = cut(got_aug[e], sub * rows, b_count)
-        near, back = tile(own_units[e], cut(own_aug[e], sub * rows, a_count), b_units, b_aug)
+        near, back = tile(
+            own_units[e].reshape(rows, width), cut(own_aug[e], sub * rows, a_count), b_units, b_aug
+        )
         back_own[e] = back
         for u in range(others):
-            for copy in sub_copies(e, others - 1 - u):
-                copy.wait_recv()
+            for v in range(mates):
+                far_share(e, u, mates - 1 - v).wait_recv()
             more, back = tile(
-                far_units[u, e], cut(far_aug[u, e], sub_of(u) * rows, a_count), b_units, b_aug
+                far_units[u, e].reshape(rows, width),
+                cut(far_aug[u, e], sub_of(u) * rows, a_count),
+                b_units,
+                b_aug,
             )
             near = near + more
             back_send[u, e] = back.astype(jnp.bfloat16)
@@ -273,14 +382,6 @@
 
     loop(peers, pair_step)
 
-    def count_step(b, found):
-        at = owner_ref[b] - me * blocks
-        return tuple(jnp.where(at == l, counts_ref[b], found[l]) for l in range(blocks))
-
-    own_counts = fold(
-        counts_ref.shape[0], count_step, (jnp.int32(0),) * blocks, unrolled=32
-    )
-
     def arrive(e):
         near_copy(peers - 1 - e).wait_recv()
 
@@ -296,8 +397,8 @@
 
         def add(e, total, l=l):
             own, asked = own_pair(e), asked_pair(e)
-            mine = (own[1] >= 0) & (local_of(own[0]) == l)
-            theirs = (asked[1] >= 0) & (local_of(asked[1]) == l)
+            mine = (own[1] >= 0) & (own_local(e) == l)
+            theirs = (asked[1] >= 0) & (asked_local(e) == l)
             part = back_own[e]
             for u in range(others):
                 part = part + back_got[u, e].astype(jnp.float32)
@@ -308,15 +409,19 @@
         numer = aff_ref[l].astype(jnp.float32) + total[0:cols]
         denom = 1.0 + total[cols : cols + 1]
         keep = sub * rows + column < own_counts[l]
-        out_ref[l] = jnp.where(keep, numer / denom, 0.0).astype(jnp.bfloat16)
+        out_ref[l] = jnp.where(keep, numer * (1.0 / denom), 0.0).astype(jnp.bfloat16)
 
     def sent(e):
         table_copy(e).wait_send()
         near_copy(e).wait_send()
         for copy in pair_copies(e):
             copy.wait_send()
+        for v in range(mates):
+            got_share(e, v).wait_send()
 
         def sub_sent(u):
+            for v in range(mates):
+                far_share(e, u, v).wait_send()
             back_copy(e, u).wait_send()
             for copy in sub_copies(e, u):
                 copy.wait_send()
@@ -329,29 +434,37 @@
 def on_device(vectors, affinity, counts, owner_map, pair_table):
     pair_count = lax.axis_size("pairs")
     sub_count = lax.axis_size("sub")
+    core_count = lax.axis_size("feat")
     blocks, rows, width = vectors.shape
     cols = affinity.shape[2]
     height = cols + 16
-    peers, others = pair_count - 1, sub_count - 1
+    peers, others, mates = pair_count - 1, sub_count - 1, core_count - 1
+    part = rows // core_count
+    parts = (core_count, part, width)
     slots = pair_table.shape[0]
     table = pair_table.T
     half = jnp.bfloat16
     dma = pltpu.SemaphoreType.DMA
     vmem = pl.BlockSpec(memory_space=pltpu.VMEM)
-    smem = pl.BlockSpec(memory_space=pltpu.SMEM)
+    hbm = pl.BlockSpec(memory_space=pltpu.HBM)
     out = pl.pallas_call(
-        functools.partial(kernel, pair_count, sub_count),
+        functools.partial(kernel, pair_count, sub_count, core_count),
         out_shape=jax.ShapeDtypeStruct((blocks, cols, rows), half),
-        in_specs=[vmem, vmem, smem, smem, smem, vmem],
+        in_specs=[hbm] * 5,
         out_specs=vmem,
         scratch_shapes=[
-            pltpu.VMEM((peers, rows, width), half),
+            pltpu.VMEM((blocks,) + parts, half),
+            pltpu.VMEM((blocks, cols, rows), half),
+            pltpu.SMEM(counts.shape, jnp.int32),
+            pltpu.SMEM(owner_map.shape, jnp.int32),
+            pltpu.SMEM((2, slots), jnp.int32),
+            pltpu.VMEM((peers,) + parts, half),
             pltpu.VMEM((peers, height, rows), half),
-            pltpu.VMEM((others, peers, rows, width), half),
+            pltpu.VMEM((others, peers) + parts, half),
             pltpu.VMEM((others, peers, height, rows), half),
-            pltpu.VMEM((peers, rows, width), half),
+            pltpu.VMEM((peers, part, width), half),
             pltpu.VMEM((peers, height, rows), half),
-            pltpu.VMEM((peers, rows, width), half),
+            pltpu.VMEM((peers,) + parts, half),
             pltpu.VMEM((peers, height, rows), half),
             pltpu.VMEM((peers, height, rows), half),
             pltpu.VMEM((peers, height, rows), half),
@@ -360,6 +473,7 @@
             pltpu.VMEM((others, peers, height, rows), half),
             pltpu.VMEM((peers, 2, slots), jnp.int32),
             pltpu.SMEM((peers, 2, slots), jnp.int32),
+            dma((5,)),
             dma((peers,)),
             dma((peers,)),
             dma(()),
@@ -371,12 +485,22 @@
             dma((peers,)),
             dma((others, peers)),
             dma((others, peers)),
+            dma((others, peers, mates)),
+            dma((others, peers, mates)),
+            dma((peers, mates)),
+            dma((peers, mates)),
         ],
         compiler_params=pltpu.CompilerParams(
-            collective_id=0, has_side_effects=True, vmem_limit_bytes=50 * 1024 * 1024
+            collective_id=0, has_side_effects=True, vmem_limit_bytes=62 * 1024 * 1024
         ),
         name="pair_sums",
-    )(vectors, affinity.transpose(0, 2, 1), counts, owner_map, table, table)
+    )(
+        vectors.reshape((blocks,) + parts),
+        affinity.transpose(0, 2, 1),
+        counts,
+        owner_map,
+        table,
+    )
     return out.transpose(0, 2, 1)
 
 

time: 41.4 us -> 29.3 us (0.71)
  Pallas kernels: 36.3 us -> 27.5 us
  local copies, waits for them, and re-layouts: 4.91 us -> 1.62 us
    pallas_call x1, Pallas kernels: 36.3 us -> 27.5 us  [on_device(): pl.pallas_call(functools.partial(kernel, pair_count, sub_count, core_coun...]
    unnamed x11 -> x1, local copies, waits for them, and re-layouts: 4.91 us -> 1.62 us
where the time goes in v2:
time: 29.3 us; the launch traced here: 29.1 us
  Pallas kernels  27.5 us (94%)
  local copies, waits for them, and re-layouts  1.62 us (6%)
    pallas_call x1, Pallas kernels, on_device(): pl.pallas_call(functools.partial(kernel, pair_count, sub_count, core_coun...  27.5 us
    unnamed x1, local copies, waits for them, and re-layouts  1.62 us

profile of v2, /device:TPU:0, one launch (start us, length us, event | category | flops | bytes accessed | tf_op | source)
XLA Modules:
  0.0 29.1 jit_solution(13305573711848811055)
XLA Ops:
  0.0 27.5 %pair_sums.1 = bf16[8,32,320]{2,1,0:T(8,128)(2,1)} custom-call(bf16[8,2,160,256]{3,2,1,0:T(8,128)(2,1)} %bitcast.4, bf16[8,32,320]{2,1,0:T(8,128)(2,1)} %bitcast.6, s32[32]{0:T(128)} %counts_hbm.1, s32[32]{0:T(128)} %owner_hbm.1, s32[2,3]{1,0:T(2,128)} %bitcast.7), custom_call_target="tpu_custom_call" | custom-call | tf_op jit(solution)/shard_map/pair_sums/pallas_call | solution.py:450
  27.5 1.6 %copy.7 = bf16[8,320,32]{1,2,0:T(8,128)(2,1)} copy(bf16[8,320,32]{1,2,0:T(8,128)(2,1)} %bitcast.5) | data formatting | bytes 327680

commit v3 on v2

--- a/solution.py
+++ b/solution.py
@@ -48,13 +48,13 @@
     owner_ref,
     table_ref,
     own_units,
-    own_aug,
+    own_aff,
     far_units,
-    far_aug,
+    far_aff,
     send_units,
-    send_aug,
+    send_aff,
     got_units,
-    got_aug,
+    got_aff,
     near_send,
     near_got,
     back_own,
@@ -86,7 +86,7 @@
     rows = part * core_count
     cols = aff_ref.shape[1]
     mates = core_count - 1
-    height = own_aug.shape[1]
+    height = back_own.shape[1]
     slots = table_ref.shape[1]
     peers = pair_count - 1
     others = sub_count - 1
@@ -124,10 +124,10 @@
         return known[name, e]
 
     def own_pair(e):
-        return once("own", e, lambda: find(lambda i, k: table_ref[i, k], peer_of(e)))
+        return once("own", e, lambda: find(lambda i, k: tables[e, i, k], me)[::-1])
 
     def asked_pair(e):
-        return once("asked", e, lambda: find(lambda i, k: tables[e, i, k], me))
+        return once("asked", e, lambda: find(lambda i, k: table_ref[i, k], peer_of(e))[::-1])
 
     def own_local(e):
         return once("own at", e, lambda: local_of(own_pair(e)[0]))
@@ -140,9 +140,8 @@
         scale = lax.rsqrt(jnp.sum(floats * floats, axis=1, keepdims=True) + 1e-06)
         return (floats * scale).astype(jnp.bfloat16)
 
-    def fill_aug(block, aug_ref, e):
-        aug_ref[e, 0:cols, :] = aff_ref[block]
-        aug_ref[e, cols:height, :] = jnp.ones((height - cols, rows), jnp.bfloat16)
+    def fill_aff(block, to_ref, e):
+        to_ref[e] = aff_ref[block]
 
     def remote(src, dst, send_sem, got_sem, device):
         return pltpu.make_async_remote_copy(
@@ -176,8 +175,8 @@
                 to,
             ),
             remote(
-                own_aug.at[e],
-                far_aug.at[there, e],
+                own_aff.at[e],
+                far_aff.at[there, e],
                 sub_send_sem.at[1, u, e],
                 sub_got_sem.at[1, there, e],
                 to,
@@ -196,8 +195,8 @@
                 to,
             ),
             remote(
-                send_aug.at[e],
-                got_aug.at[there],
+                send_aff.at[e],
+                got_aff.at[there],
                 pair_send_sem.at[1, e],
                 pair_got_sem.at[1, there],
                 to,
@@ -275,17 +274,32 @@
 
     loop(others, greet_sub)
     loop(mates, greet_mate)
-    pl.semaphore_wait(barrier, peers + others + mates)
-
-    loop(peers, lambda e: table_copy(e).start())
     for fetch in fetches:
         fetch.wait()
 
+    def fill_pair(e):
+        send_units[e] = unit(vec_ref[asked_local(e), core])
+        fill_aff(asked_local(e), send_aff, e)
+
+    loop(peers, fill_pair)
+    pl.semaphore_wait(barrier, peers + others + mates)
+
+    loop(peers, lambda e: table_copy(e).start())
+
+    def start_pair(e):
+        for copy in pair_copies(e):
+            copy.start()
+
+    loop(peers, start_pair)
+
+    loop(peers, lambda e: table_copy(peers - 1 - e).wait_recv())
+    to_scalars = pltpu.make_async_copy(tables_vec, tables, tab_local_sem)
+    to_scalars.start()
+    to_scalars.wait()
+
     def start_own(e):
-        own_units[e] = unit(vec_ref[own_local(e)].reshape(rows, width)).reshape(
-            core_count, part, width
-        )
-        fill_aug(own_local(e), own_aug, e)
+        own_units[e, core] = unit(vec_ref[own_local(e), core])
+        fill_aff(own_local(e), own_aff, e)
 
         def send(u):
             for copy in sub_copies(e, u):
@@ -295,21 +309,11 @@
 
     loop(peers, start_own)
 
-    def table_in(e):
-        table_copy(peers - 1 - e).wait_recv()
-
-    loop(peers, table_in)
-    to_scalars = pltpu.make_async_copy(tables_vec, tables, tab_local_sem)
-    to_scalars.start()
-    to_scalars.wait()
-
-    def start_pair(e):
-        send_units[e] = unit(vec_ref[asked_local(e), core])
-        fill_aug(asked_local(e), send_aug, e)
-        for copy in pair_copies(e):
-            copy.start()
-
-    loop(peers, start_pair)
+    def fill_rest(e):
+        for v in range(mates):
+            own_units[e, mate_of(v)] = unit(vec_ref[own_local(e), mate_of(v)])
+
+    loop(peers, fill_rest)
 
     def count_step(b, found):
         at = owner_ref[b] - me * blocks
@@ -333,13 +337,15 @@
             got_share(e, v).start()
 
     loop(peers, share_far)
-    loop(peers, share_got)
 
     lane = lax.broadcasted_iota(jnp.int32, (height, rows), 1)
 
-    def cut(aug, first_row, count):
+    def cut(aff, first_row, count):
         keep = first_row + lane < count
-        return jnp.where(keep, aug.astype(jnp.float32), 0.0).astype(jnp.bfloat16)
+        full = jnp.concatenate(
+            [aff.astype(jnp.float32), jnp.ones((height - cols, rows), jnp.float32)], axis=0
+        )
+        return jnp.where(keep, full, 0.0).astype(jnp.bfloat16)
 
     def tile(a_units, a_aug, b_units, b_aug):
         cosine = lax.dot_general(
@@ -360,9 +366,9 @@
         for v in range(mates):
             got_share(e, mates - 1 - v).wait_recv()
         b_units = got_units[e].reshape(rows, width)
-        b_aug = cut(got_aug[e], sub * rows, b_count)
+        b_aug = cut(got_aff[e], sub * rows, b_count)
         near, back = tile(
-            own_units[e].reshape(rows, width), cut(own_aug[e], sub * rows, a_count), b_units, b_aug
+            own_units[e].reshape(rows, width), cut(own_aff[e], sub * rows, a_count), b_units, b_aug
         )
         back_own[e] = back
         for u in range(others):
@@ -370,7 +376,7 @@
                 far_share(e, u, mates - 1 - v).wait_recv()
             more, back = tile(
                 far_units[u, e].reshape(rows, width),
-                cut(far_aug[u, e], sub_of(u) * rows, a_count),
+                cut(far_aff[u, e], sub_of(u) * rows, a_count),
                 b_units,
                 b_aug,
             )
@@ -380,7 +386,22 @@
         near_send[e] = near.astype(jnp.bfloat16)
         near_copy(e).start()
 
-    loop(peers, pair_step)
+    if peers > 0:
+        share_got(0)
+
+    def pair_turn(e):
+        if isinstance(e, int):
+            if e + 1 < peers:
+                share_got(e + 1)
+        else:
+
+            @pl.when(e + 1 < peers)
+            def _():
+                share_got(e + 1)
+
+        pair_step(e)
+
+    loop(peers, pair_turn)
 
     def arrive(e):
         near_copy(peers - 1 - e).wait_recv()
@@ -459,13 +480,13 @@
             pltpu.SMEM(owner_map.shape, jnp.int32),
             pltpu.SMEM((2, slots), jnp.int32),
             pltpu.VMEM((peers,) + parts, half),
-            pltpu.VMEM((peers, height, rows), half),
+            pltpu.VMEM((peers, cols, rows), half),
             pltpu.VMEM((others, peers) + parts, half),
-            pltpu.VMEM((others, peers, height, rows), half),
+            pltpu.VMEM((others, peers, cols, rows), half),
             pltpu.VMEM((peers, part, width), half),
-            pltpu.VMEM((peers, height, rows), half),
+            pltpu.VMEM((peers, cols, rows), half),
             pltpu.VMEM((peers,) + parts, half),
-            pltpu.VMEM((peers, height, rows), half),
+            pltpu.VMEM((peers, cols, rows), half),
             pltpu.VMEM((peers, height, rows), half),
             pltpu.VMEM((peers, height, rows), half),
             pltpu.VMEM((peers, height, rows), jnp.float32),

time: 29.3 us -> 27.6 us (0.942)
  Pallas kernels: 27.5 us -> 25.8 us
    pallas_call x1, Pallas kernels: 27.5 us -> 25.8 us  [on_device(): pl.pallas_call(functools.partial(kernel, pair_count, sub_count, core_coun...]
where the time goes in v3:
time: 27.6 us; the launch traced here: 27.4 us
  Pallas kernels  25.8 us (93%)
  local copies, waits for them, and re-layouts  1.62 us (6%)
    pallas_call x1, Pallas kernels, on_device(): pl.pallas_call(functools.partial(kernel, pair_count, sub_count, core_coun...  25.8 us
    unnamed x1, local copies, waits for them, and re-layouts  1.62 us

profile of v3, /device:TPU:0, one launch (start us, length us, event | category | flops | bytes accessed | tf_op | source)
XLA Modules:
  0.0 27.4 jit_solution(10503271467918033297)
XLA Ops:
  0.0 25.8 %pair_sums.1 = bf16[8,32,320]{2,1,0:T(8,128)(2,1)} custom-call(bf16[8,2,160,256]{3,2,1,0:T(8,128)(2,1)} %bitcast.4, bf16[8,32,320]{2,1,0:T(8,128)(2,1)} %bitcast.6, s32[32]{0:T(128)} %counts_hbm.1, s32[32]{0:T(128)} %owner_hbm.1, s32[2,3]{1,0:T(2,128)} %bitcast.7), custom_call_target="tpu_custom_call" | custom-call | tf_op jit(solution)/shard_map/pair_sums/pallas_call | solution.py:471
  25.8 1.6 %copy.7 = bf16[8,320,32]{1,2,0:T(8,128)(2,1)} copy(bf16[8,320,32]{1,2,0:T(8,128)(2,1)} %bitcast.5) | data formatting | bytes 327680

commit v4 on v3

--- a/solution.py
+++ b/solution.py
@@ -55,17 +55,16 @@
     send_aff,
     got_units,
     got_aff,
+    near_sum,
     near_send,
     near_got,
     back_own,
     back_send,
     back_got,
-    tables_vec,
     tables,
     fetch_sem,
     tab_send_sem,
     tab_got_sem,
-    tab_local_sem,
     sub_send_sem,
     sub_got_sem,
     pair_send_sem,
@@ -156,8 +155,8 @@
     def table_copy(e):
         there = peers - 1 - e
         return remote(
-            table_hbm,
-            tables_vec.at[there],
+            table_ref,
+            tables.at[there],
             tab_send_sem.at[e],
             tab_got_sem.at[there],
             {"pairs": peer_of(e)},
@@ -293,9 +292,6 @@
     loop(peers, start_pair)
 
     loop(peers, lambda e: table_copy(peers - 1 - e).wait_recv())
-    to_scalars = pltpu.make_async_copy(tables_vec, tables, tab_local_sem)
-    to_scalars.start()
-    to_scalars.wait()
 
     def start_own(e):
         own_units[e, core] = unit(vec_ref[own_local(e), core])
@@ -336,7 +332,7 @@
         for v in range(mates):
             got_share(e, v).start()
 
-    loop(peers, share_far)
+    loop(peers, share_got)
 
     lane = lax.broadcasted_iota(jnp.int32, (height, rows), 1)
 
@@ -358,50 +354,63 @@
         back = jnp.dot(b_aug, rounded, preferred_element_type=jnp.float32)
         return near, back
 
-    def pair_step(e):
+    def live_counts(e):
         first, second = own_pair(e)
         live = second >= 0
-        a_count = jnp.where(live, counts_ref[jnp.maximum(first, 0)], 0)
-        b_count = jnp.where(live, counts_ref[jnp.maximum(second, 0)], 0)
+        return (
+            jnp.where(live, counts_ref[jnp.maximum(first, 0)], 0),
+            jnp.where(live, counts_ref[jnp.maximum(second, 0)], 0),
+        )
+
+    def own_step(e):
+        a_count, b_count = live_counts(e)
+        a_aug = cut(own_aff[e], sub * rows, a_count)
         for v in range(mates):
             got_share(e, mates - 1 - v).wait_recv()
-        b_units = got_units[e].reshape(rows, width)
+        near_sum[e], back_own[e] = tile(
+            own_units[e].reshape(rows, width),
+            a_aug,
+            got_units[e].reshape(rows, width),
+            cut(got_aff[e], sub * rows, b_count),
+        )
+
+    def far_step(e):
+        a_count, b_count = live_counts(e)
         b_aug = cut(got_aff[e], sub * rows, b_count)
-        near, back = tile(
-            own_units[e].reshape(rows, width), cut(own_aff[e], sub * rows, a_count), b_units, b_aug
-        )
-        back_own[e] = back
+        near = near_sum[e]
         for u in range(others):
+            a_aug = cut(far_aff[u, e], sub_of(u) * rows, a_count)
             for v in range(mates):
                 far_share(e, u, mates - 1 - v).wait_recv()
             more, back = tile(
                 far_units[u, e].reshape(rows, width),
-                cut(far_aff[u, e], sub_of(u) * rows, a_count),
-                b_units,
+                a_aug,
+                got_units[e].reshape(rows, width),
                 b_aug,
             )
-            near = near + more
             back_send[u, e] = back.astype(jnp.bfloat16)
             back_copy(e, u).start()
+            near = near + more
         near_send[e] = near.astype(jnp.bfloat16)
         near_copy(e).start()
 
+    loop(peers, own_step)
     if peers > 0:
-        share_got(0)
-
-    def pair_turn(e):
+        share_far(0)
+
+    def far_turn(e):
         if isinstance(e, int):
             if e + 1 < peers:
-                share_got(e + 1)
+                share_far(e + 1)
         else:
 
             @pl.when(e + 1 < peers)
             def _():
-                share_got(e + 1)
-
-        pair_step(e)
-
-    loop(peers, pair_turn)
+                share_far(e + 1)
+
+        far_step(e)
+
+    loop(peers, far_turn)
 
     def arrive(e):
         near_copy(peers - 1 - e).wait_recv()
@@ -487,17 +496,16 @@
             pltpu.VMEM((peers, cols, rows), half),
             pltpu.VMEM((peers,) + parts, half),
             pltpu.VMEM((peers, cols, rows), half),
+            pltpu.VMEM((peers, height, rows), jnp.float32),
             pltpu.VMEM((peers, height, rows), half),
             pltpu.VMEM((peers, height, rows), half),
             pltpu.VMEM((peers, height, rows), jnp.float32),
             pltpu.VMEM((others, peers, height, rows), half),
             pltpu.VMEM((others, peers, height, rows), half),
-            pltpu.VMEM((peers, 2, slots), jnp.int32),
             pltpu.SMEM((peers, 2, slots), jnp.int32),
             dma((5,)),
             dma((peers,)),
             dma((peers,)),
-            dma(()),
             dma((2, others, peers)),
             dma((2, others, peers)),
             dma((2, peers)),

time: 27.6 us -> 27 us (0.978)
  Pallas kernels: 25.8 us -> 25.2 us
    pallas_call x1, Pallas kernels: 25.8 us -> 25.2 us  [on_device(): pl.pallas_call(functools.partial(kernel, pair_count, sub_count, core_coun...]
where the time goes in v4:
time: 27 us; the launch traced here: 26.9 us
  Pallas kernels  25.2 us (93%)
  local copies, waits for them, and re-layouts  1.62 us (6%)
    pallas_call x1, Pallas kernels, on_device(): pl.pallas_call(functools.partial(kernel, pair_count, sub_count, core_coun...  25.2 us
    unnamed x1, local copies, waits for them, and re-layouts  1.62 us

profile of v4, /device:TPU:0, one launch (start us, length us, event | category | flops | bytes accessed | tf_op | source)
XLA Modules:
  0.0 26.9 jit_solution(10418401827319054971)
XLA Ops:
  0.0 25.2 %pair_sums.1 = bf16[8,32,320]{2,1,0:T(8,128)(2,1)} custom-call(bf16[8,2,160,256]{3,2,1,0:T(8,128)(2,1)} %bitcast.4, bf16[8,32,320]{2,1,0:T(8,128)(2,1)} %bitcast.6, s32[32]{0:T(128)} %counts_hbm.1, s32[32]{0:T(128)} %owner_hbm.1, s32[2,3]{1,0:T(2,128)} %bitcast.7), custom_call_target="tpu_custom_call" | custom-call | tf_op jit(solution)/shard_map/pair_sums/pallas_call | solution.py:480
  25.3 1.6 %copy.7 = bf16[8,320,32]{1,2,0:T(8,128)(2,1)} copy(bf16[8,320,32]{1,2,0:T(8,128)(2,1)} %bitcast.5) | data formatting | bytes 327680

commit v5 on v4

--- a/solution.py
+++ b/solution.py
@@ -333,6 +333,8 @@
             got_share(e, v).start()
 
     loop(peers, share_got)
+    if peers > 0:
+        share_far(0)
 
     lane = lax.broadcasted_iota(jnp.int32, (height, rows), 1)
 
@@ -395,8 +397,6 @@
         near_copy(e).start()
 
     loop(peers, own_step)
-    if peers > 0:
-        share_far(0)
 
     def far_turn(e):
         if isinstance(e, int):

time: 27 us -> 26.1 us (0.967)
  Pallas kernels: 25.2 us -> 24.3 us
    pallas_call x1, Pallas kernels: 25.2 us -> 24.3 us  [on_device(): pl.pallas_call(functools.partial(kernel, pair_count, sub_count, core_coun...]
where the time goes in v5:
time: 26.1 us; the launch traced here: 25.9 us
  Pallas kernels  24.3 us (93%)
  local copies, waits for them, and re-layouts  1.62 us (6%)
    pallas_call x1, Pallas kernels, on_device(): pl.pallas_call(functools.partial(kernel, pair_count, sub_count, core_coun...  24.3 us
    unnamed x1, local copies, waits for them, and re-layouts  1.62 us

profile of v5, /device:TPU:0, one launch (start us, length us, event | category | flops | bytes accessed | tf_op | source)
XLA Modules:
  0.0 25.9 jit_solution(11462395379226687070)
XLA Ops:
  0.0 24.3 %pair_sums.1 = bf16[8,32,320]{2,1,0:T(8,128)(2,1)} custom-call(bf16[8,2,160,256]{3,2,1,0:T(8,128)(2,1)} %bitcast.4, bf16[8,32,320]{2,1,0:T(8,128)(2,1)} %bitcast.6, s32[32]{0:T(128)} %counts_hbm.1, s32[32]{0:T(128)} %owner_hbm.1, s32[2,3]{1,0:T(2,128)} %bitcast.7), custom_call_target="tpu_custom_call" | custom-call | tf_op jit(solution)/shard_map/pair_sums/pallas_call | solution.py:480
  24.3 1.6 %copy.7 = bf16[8,320,32]{1,2,0:T(8,128)(2,1)} copy(bf16[8,320,32]{1,2,0:T(8,128)(2,1)} %bitcast.5) | data formatting | bytes 327680
